TPU v7x, 512 devices: a whole 4x4x16 slice. The times are simulated.
512 devices in a mesh: lat: 32 (over z_lo, x), lon: 16 (over y, z_hi, core).
Axes of the slice: x: 4, y: 4, z: 16 (z_hi: 2, z_lo: 8; z = z_hi * 8 + z_lo), core: 2. Of those that a mesh axis runs over, the one named last changes fastest.
Arguments:
- grid_field: bfloat16 [512, 2880, 64], P('lat', 'lon'), may hold values from -6 to 6
- disco_reach: int32 [512], P('lat'), may hold values from 1 to 20, as said below
- disco_taps: float32 [512, 492], P('lat'), may hold values from -1 to 1
- disco_weight: bfloat16 [4, 64, 64], replicated, may hold values from -0.375 to 0.375
- legendre: bfloat16 [512, 32, 768], P('lat', 'lon'), may hold values from -0.25 to 0.25
- spectral_mixing_weight: bfloat16 [768, 2, 64, 64], P('lat'), may hold values from -0.5 to 0.5
Outputs:
- block_out: bfloat16 [512, 2880, 64], P('lat', 'lon')
Inputs may be any that keep to these rules, and one draw needn't show every extreme that they name: `disco_reach`: the rows at both poles reach 20.
All inputs are finite; a program needn't handle non-finite values.
Results may differ from a plain program's by a relative error of at most 0.02.
Values may be sent and summed in bfloat16 or wider, within the bound.
No kernel may reach another device: no remote copies, remote signals or barrier semaphores. Data moves between devices by JAX's collectives and lax.ppermute only.
A program may use at most 128 MiB of HBM per device.

v0:
```python
import math
import jax
import jax.numpy as jnp
from jax import lax
from jax.sharding import PartitionSpec as P

NLON = 2880
HMAX = 20
BASES = 4


def padded(cells, sides, width, closed):
    for axis, dim in sides:
        count = lax.axis_size(axis)
        ends = count if closed else count - 1
        head = lax.slice_in_dim(cells, 0, width, axis=dim)
        tail = lax.slice_in_dim(cells, cells.shape[dim] - width, cells.shape[dim], axis=dim)
        cells = jnp.concatenate(
            [
                lax.ppermute(tail, axis, [(i, (i + 1) % count) for i in range(ends)]),
                cells,
                lax.ppermute(head, axis, [((i + 1) % count, i) for i in range(ends)]),
            ],
            axis=dim,
        )
    return cells


def angles(columns, orders):
    residues = columns[:, None] * orders[None, :] % NLON
    return residues.astype(jnp.float32) * (2.0 * math.pi / NLON)


def forward_table(columns, orders):
    phases = angles(columns, orders)
    factor = 1.0 / math.sqrt(NLON)
    return jnp.stack([jnp.cos(phases) * factor, -jnp.sin(phases) * factor], axis=1).astype(
        jnp.bfloat16
    )


def inverse_table(orders, columns, mode_count):
    phases = angles(columns, orders)
    factor = 1.0 / math.sqrt(mode_count)
    return jnp.stack([jnp.cos(phases).T * factor, -jnp.sin(phases).T * factor], axis=0).astype(
        jnp.bfloat16
    )


def disco(grid_field, disco_reach, disco_taps, disco_weight):
    lat_rows, lon_cols, channels = grid_field.shape
    tap_count = 2 * HMAX + 1
    widened = padded(grid_field, (("lon", 1),), HMAX, True)
    extended = padded(widened, (("lat", 0),), 1, False)
    flattened = extended.reshape(lat_rows + 2, (lon_cols + 2 * HMAX) * channels)
    offsets = jnp.abs(jnp.arange(tap_count, dtype=jnp.int32) - HMAX)
    within = offsets[None, :] <= disco_reach[:, None]
    kernel_coef = jnp.where(
        within[:, None, None, :], disco_taps.reshape(lat_rows, BASES, 3, tap_count), 0.0
    )
    running_totals = [
        jnp.zeros((lat_rows, lon_cols * channels), jnp.float32) for kernel in range(BASES)
    ]
    for lat_step in range(3):
        for lon_step in range(tap_count):
            window = flattened[
                lat_step : lat_step + lat_rows,
                lon_step * channels : (lon_step + lon_cols) * channels,
            ].astype(jnp.float32)
            for kernel in range(BASES):
                running_totals[kernel] = (
                    running_totals[kernel]
                    + kernel_coef[:, kernel, lat_step, lon_step][:, None] * window
                )
    basis_sums = (
        jnp.stack(running_totals, axis=1)
        .astype(jnp.bfloat16)
        .reshape(lat_rows, BASES, lon_cols, channels)
    )
    return jnp.einsum("rkjc,kcd->rjd", basis_sums, disco_weight, preferred_element_type=jnp.float32)


def per_device(grid_field, disco_reach, disco_taps, disco_weight, legendre, spectral_mixing_weight):
    lat_rows, lon_cols, channels = grid_field.shape
    orders_dev = legendre.shape[1]
    lon_count = lax.axis_size("lon")
    lat_count = lax.axis_size("lat")
    mode_count = orders_dev * lon_count
    harmonic_degree_rows = legendre.shape[2] // lat_count
    lon_place = lax.axis_index("lon")
    disco_out = disco(grid_field, disco_reach, disco_taps, disco_weight)
    mode_index = jnp.arange(mode_count, dtype=jnp.int32)
    own_columns = lon_place * lon_cols + jnp.arange(lon_cols, dtype=jnp.int32)
    full_table = forward_table(jnp.arange(NLON, dtype=jnp.int32), mode_index)
    row_spectra = jnp.einsum(
        "blv,lis->bsiv",
        lax.all_to_all(grid_field, "lon", split_axis=0, concat_axis=1, tiled=True),
        full_table,
        preferred_element_type=jnp.float32,
    ).astype(jnp.bfloat16)
    spectra = lax.all_to_all(row_spectra, "lon", split_axis=1, concat_axis=0, tiled=True).reshape(
        lat_rows, orders_dev, 2 * channels
    )
    orders_global = lon_place * orders_dev + jnp.arange(orders_dev, dtype=jnp.int32)

    def masked(amount):
        degree = jnp.arange(amount, dtype=jnp.int32)
        within = degree[None, :] >= orders_global[:, None]
        return jnp.where(within[None], legendre, jnp.zeros((), jnp.bfloat16))

    coeffs = lax.psum_scatter(
        jnp.einsum(
            "iml,imc->lmc",
            masked(harmonic_degree_rows * lax.axis_size("lat")),
            spectra,
            preferred_element_type=jnp.float32,
        ).astype(jnp.bfloat16),
        "lat",
        scatter_dimension=0,
        tiled=True,
    )
    real_part = spectral_mixing_weight[:, 0]
    imag_part = spectral_mixing_weight[:, 1]
    upper = jnp.concatenate([real_part, imag_part], axis=2)
    lower = jnp.concatenate([-imag_part, real_part], axis=2)
    complex_block = jnp.concatenate([upper, lower], axis=1)
    mixed_modes = jnp.einsum(
        "lmc,lcd->lmd", coeffs, complex_block, preferred_element_type=jnp.float32
    ).astype(jnp.bfloat16)
    portion = lax.all_gather(mixed_modes, "lat", axis=0, tiled=True)
    grid_modes = jnp.einsum(
        "iml,lmc->imc", masked(portion.shape[0]), portion, preferred_element_type=jnp.float32
    ).astype(jnp.bfloat16)
    own_inverse = inverse_table(mode_index, own_columns, mode_count)
    portion = lax.all_gather(grid_modes, "lon", axis=1, tiled=True)
    amount = portion.shape[1]
    shaped = portion.reshape(lat_rows, amount, 2, channels)
    spectral_out = jnp.einsum(
        "impc,pmj->ijc", shaped, own_inverse, preferred_element_type=jnp.float32
    ).astype(jnp.bfloat16)
    combined = spectral_out.astype(jnp.float32) + disco_out
    return (grid_field.astype(jnp.float32) + jax.nn.gelu(combined, approximate=True)).astype(
        jnp.bfloat16
    )


def solution(mesh):
    in_specs = (
        P("lat", "lon", None),
        P("lat"),
        P("lat", None),
        P(),
        P("lat", "lon", None),
        P("lat", None, None, None),
    )
    out_specs = P("lat", "lon", None)
    return jax.shard_map(
        per_device, mesh=mesh, in_specs=in_specs, out_specs=out_specs, check_vma=False
    )
```

profile of v0, /device:TPU:1, one launch (start us, length us, event | category | flops | bytes accessed | tf_op | source)
XLA Modules:
  0.0 830.0 jit_solution(7017814243375401134)
XLA Ops:
  6.5 19.4 %all-to-all-start = ((bf16[16,180,64]{1,2,0:T(8,128)(2,1)}), bf16[16,180,64]{1,2,0:T(8,128)(2,1)S(1)}, u32[]{:S(2)}, u32[]{:S(2)}) async-start(bf16[16,180,64]{1,2,0:T(8,128)(2,1)} %param.6), calls=%async_computation | async-start | bytes 1048576 | tf_op jit(solution)/shard_map/all_to_all | solution.py:97
  26.8 12.2 %collective-permute-start = (bf16[16,20,64]{1,2,0:T(8,128)(2,1)}, bf16[16,20,64]{1,2,0:T(8,128)(2,1)S(1)}, u32[]{:S(2)}, u32[]{:S(2)}) collective-permute-start(bf16[16,20,64]{1,2,0:T(8,128)(2,1)} %get-tuple-element.501), channel_id=1, source_target_pairs={{0,1},{1,2},{2,3},{3,4},{4,5},{5,6},{6,7},{7,8},{8,9},{9,10},{10,1... | collective-permute-start | bytes 122888 | tf_op jit(solution)/shard_map/ppermute | solution.py:20
  39.0 1.9 collective-permute-start.1
  41.3 1.5 slice_reduce_fusion.486
  42.8 1.4 slice_reduce_fusion.491
  44.2 1.5 slice_reduce_fusion.490
  45.7 1.5 slice_reduce_fusion.489
  47.2 1.5 slice_reduce_fusion.488
  48.7 1.5 slice_reduce_fusion.487
  50.1 1.3 slice_reduce_fusion.485
  51.4 1.5 slice_reduce_fusion.363
  53.0 1.5 slice_reduce_fusion.362
  54.5 1.5 slice_reduce_fusion.361
  55.9 1.5 slice_reduce_fusion.360
  57.4 1.5 slice_reduce_fusion.359
  58.9 1.4 slice_reduce_fusion.358
  60.3 1.3 slice_reduce_fusion.357
  61.6 1.5 slice_reduce_fusion.235
  63.1 1.5 slice_reduce_fusion.234
  64.6 1.7 slice_reduce_fusion.233
  66.3 1.5 slice_reduce_fusion.232
  67.7 1.5 slice_reduce_fusion.231
  69.2 1.5 slice_reduce_fusion.230
  70.7 1.5 slice_reduce_fusion.107
  72.2 1.5 slice_reduce_fusion.106
  73.6 1.5 slice_reduce_fusion.105
  75.1 1.5 slice_reduce_fusion.104
  76.6 1.5 slice_reduce_fusion.103
  78.1 2.3 multiply_convert_fusion
  82.5 1.3 slice_reduce_fusion.229
  83.9 3.1 collective-permute-start.2
  87.0 1.7 collective-permute-start.3
  88.7 1.3 slice_reduce_fusion.102
  90.0 1.3 dynamic-slice
  94.5 32.1 %fusion.533 = bf16[16,11520]{1,0:T(8,128)(2,1)S(1)} fusion(f32[16]{0:T(128)S(1)} %copy-done.117, f32[16]{0:T(128)S(1)} %copy-done.118, f32[16]{0:T(128)S(1)} %copy-done.119, f32[16]{0:T(128)S(1)} %copy-done.120, f32[16]{0:T(128)S(1)} %copy-done.121, f32[16]{0:T(128)S(1)} %copy-done.122, f32[16]{0:T(128)S(1)} %copy-done.123, f32[16]{0:T(128)S(1)} %copy-done.124, ...), kind=kLoop, calls=%fused_computation.1021 | loop fusion | flops 68014080 | bytes 45719232 | tf_op jit(solution)/shard_map/convert.8
  126.7 33.0 %fusion.532 = bf16[16,11520]{1,0:T(8,128)(2,1)} fusion(f32[16]{0:T(128)S(1)} %copy-done.89, f32[16]{0:T(128)S(1)} %copy-done.90, f32[16]{0:T(128)S(1)} %copy-done.91, f32[16]{0:T(128)S(1)} %copy-done.92, f32[16]{0:T(128)S(1)} %copy-done.93, f32[16]{0:T(128)S(1)} %copy-done.94, f32[16]{0:T(128)S(1)} %copy-done.95, f32[16]{0:T(128)S(1)} %copy-done.96, ...), kind=kLoop, calls=%fused_computation.1020 | loop fusion | flops 68014080 | bytes 45719232 | tf_op jit(solution)/shard_map/convert.7
  161.2 1.3 fusion.18
  163.2 15.7 %all-to-all-start.1 = ((bf16[16,2,128]{2,1,0:T(2,128)(2,1)}), bf16[16,2,128]{2,1,0:T(2,128)(2,1)S(1)}, u32[]{:S(2)}, u32[]{:S(2)}) async-start(bf16[16,2,128]{2,1,0:T(2,128)(2,1)} %reshape.1243), calls=%async_computation.1 | async-start | bytes 16384 | tf_op jit(solution)/shard_map/all_to_all | solution.py:101
  179.4 31.8 %fusion.531 = bf16[16,11520]{1,0:T(8,128)(2,1)S(1)} fusion(f32[16]{0:T(128)S(1)} %copy-done.50, f32[16]{0:T(128)S(1)} %copy-done.51, f32[16]{0:T(128)S(1)} %copy-done.52, f32[16]{0:T(128)S(1)} %copy-done.54, f32[16]{0:T(128)S(1)} %copy-done.55, f32[16]{0:T(128)S(1)} %copy-done.56, f32[16]{0:T(128)S(1)} %copy-done.57, f32[16]{0:T(128)S(1)} %copy-done.58, ...), kind=kLoop, calls=%fused_computation.1019 | loop fusion | flops 68014080 | bytes 45719232 | tf_op jit(solution)/shard_map/convert.6
  213.6 31.9 %fusion.530 = bf16[16,11520]{1,0:T(8,128)(2,1)S(1)} fusion(f32[16]{0:T(128)S(1)} %copy-done.10, f32[16]{0:T(128)S(1)} %copy-done.11, f32[16]{0:T(128)S(1)} %copy-done.12, f32[16]{0:T(128)S(1)} %copy-done.13, f32[16]{0:T(128)S(1)} %copy-done.14, f32[16]{0:T(128)S(1)} %copy-done.15, f32[16]{0:T(128)S(1)} %copy-done.16, f32[16]{0:T(128)S(1)} %copy-done.17, ...), kind=kLoop, calls=%fused_computation.1018 | loop fusion | flops 68014080 | bytes 45719232 | tf_op jit(solution)/shard_map/convert.5
  246.9 1.2 copy.68
  248.6 1.1 copy.69
  250.2 1.1 copy.70
  251.3 384.7 %all-reduce.3.cloned.1.call-done = bf16[768,2,128]{2,1,0:T(2,128)(2,1)} async-done(((bf16[768,2,128]{2,1,0:T(2,128)(2,1)}), bf16[768,2,128]{2,1,0:T(2,128)(2,1)}) %all-reduce.3.cloned.1.call-update) | async-done | bytes 393232
  636.1 1.7 convolution_convert_fusion.2
  637.7 107.0 %all_gather.6 = bf16[768,2,128]{2,1,0:T(2,128)(2,1)S(1)} all-gather(bf16[24,2,128]{2,1,0:T(2,128)(2,1)S(1)} %convolution_convert_fusion.2), channel_id=1, replica_groups=mesh['lat'=32,'lon'=16] {'lat'}, dimensions={0}, use_global_device_ids=true | all-gather | bytes 405504 | tf_op jit(solution)/shard_map/all_gather | solution.py:130
  744.9 74.4 %all_gather.7 = bf16[16,32,128]{2,0,1:T(8,128)(2,1)S(1)} all-gather(bf16[16,2,128]{2,0,1:T(8,128)(2,1)S(1)} %fusion.19), channel_id=1, replica_groups=mesh['lat'=32,'lon'=16] {'lon'}, dimensions={1}, use_global_device_ids=true | all-gather | bytes 139264 | tf_op jit(solution)/shard_map/all_gather | solution.py:135
  819.8 2.9 fusion.32
  (296 shorter events, 12.2 us)
Async XLA Ops:
  6.5 813.2 %copy-start = (bf16[4,64,64]{2,1,0:T(8,128)(2,1)S(1)}, bf16[4,64,64]{2,1,0:T(8,128)(2,1)}, u32[]{:S(2)}) copy-start(bf16[4,64,64]{2,1,0:T(8,128)(2,1)} %param.9) | copy-start | bytes 98308
  6.5 19.4 %copy-start.1 = (bf16[16,180,64]{1,2,0:T(8,128)(2,1)S(1)}, bf16[16,180,64]{1,2,0:T(8,128)(2,1)}, u32[]{:S(2)}) copy-start(bf16[16,180,64]{1,2,0:T(8,128)(2,1)} %param.6) | copy-start | bytes 1105924
  6.5 34.4 %copy-start.9 = (f32[16,492]{1,0:T(8,128)S(1)}, f32[16,492]{1,0:T(8,128)}, u32[]{:S(2)}) copy-start(f32[16,492]{1,0:T(8,128)} %param.8) | copy-start | bytes 94468
  6.5 34.6 %copy-start.127 = (s32[16]{0:T(128)S(1)}, s32[16]{0:T(128)}, u32[]{:S(2)}) copy-start(s32[16]{0:T(128)} %param.7) | copy-start | bytes 196
  6.5 153.2 %all-to-all-start = ((bf16[16,180,64]{1,2,0:T(8,128)(2,1)}), bf16[16,180,64]{1,2,0:T(8,128)(2,1)S(1)}, u32[]{:S(2)}, u32[]{:S(2)}) async-start(bf16[16,180,64]{1,2,0:T(8,128)(2,1)} %param.6), calls=%async_computation | async-start | bytes 1048576 | tf_op jit(solution)/shard_map/all_to_all | solution.py:97
  26.8 57.0 %collective-permute-start = (bf16[16,20,64]{1,2,0:T(8,128)(2,1)}, bf16[16,20,64]{1,2,0:T(8,128)(2,1)S(1)}, u32[]{:S(2)}, u32[]{:S(2)}) collective-permute-start(bf16[16,20,64]{1,2,0:T(8,128)(2,1)} %get-tuple-element.501), channel_id=1, source_target_pairs={{0,1},{1,2},{2,3},{3,4},{4,5},{5,6},{6,7},{7,8},{8,9},{9,10},{10,1... | collective-permute-start | bytes 122888 | tf_op jit(solution)/shard_map/ppermute | solution.py:20
  39.0 44.7 %collective-permute-start.1 = (bf16[16,20,64]{1,2,0:T(8,128)(2,1)S(1)}, bf16[16,20,64]{1,2,0:T(8,128)(2,1)S(1)}, u32[]{:S(2)}, u32[]{:S(2)}) collective-permute-start(bf16[16,20,64]{1,2,0:T(8,128)(2,1)S(1)} %get-tuple-element.502), channel_id=1, source_target_pairs={{1,0},{2,1},{3,2},{4,3},{5,4},{6,5},{7,6},{8,7},{9,8},{10,9},{11,1... | collective-permute-start | bytes 122888 | tf_op jit(solution)/shard_map/ppermute | solution.py:22
  83.9 8.0 collective-permute-start.2
  87.0 4.9 collective-permute-start.3
  94.4 32.2 %copy-start.88 = (f32[16]{0:T(128)S(1)}, f32[16]{0:T(128)}, u32[]{:S(2)}) copy-start(f32[16]{0:T(128)} %get-tuple-element.133) | copy-start | bytes 196
  94.4 32.2 %copy-start.89 = (f32[16]{0:T(128)S(1)}, f32[16]{0:T(128)}, u32[]{:S(2)}) copy-start(f32[16]{0:T(128)} %get-tuple-element.144) | copy-start | bytes 196
  94.4 32.2 %copy-start.90 = (f32[16]{0:T(128)S(1)}, f32[16]{0:T(128)}, u32[]{:S(2)}) copy-start(f32[16]{0:T(128)} %get-tuple-element.145) | copy-start | bytes 196
  94.5 32.2 %copy-start.91 = (f32[16]{0:T(128)S(1)}, f32[16]{0:T(128)}, u32[]{:S(2)}) copy-start(f32[16]{0:T(128)} %get-tuple-element.146) | copy-start | bytes 196
  94.5 32.2 %copy-start.92 = (f32[16]{0:T(128)S(1)}, f32[16]{0:T(128)}, u32[]{:S(2)}) copy-start(f32[16]{0:T(128)} %get-tuple-element.147) | copy-start | bytes 196
  94.5 32.2 %copy-start.93 = (f32[16]{0:T(128)S(1)}, f32[16]{0:T(128)}, u32[]{:S(2)}) copy-start(f32[16]{0:T(128)} %get-tuple-element.148) | copy-start | bytes 196
  94.5 32.2 %copy-start.94 = (f32[16]{0:T(128)S(1)}, f32[16]{0:T(128)}, u32[]{:S(2)}) copy-start(f32[16]{0:T(128)} %get-tuple-element.149) | copy-start | bytes 196
  94.5 32.2 %copy-start.95 = (f32[16]{0:T(128)S(1)}, f32[16]{0:T(128)}, u32[]{:S(2)}) copy-start(f32[16]{0:T(128)} %get-tuple-element.150) | copy-start | bytes 196
  94.5 32.2 %copy-start.96 = (f32[16]{0:T(128)S(1)}, f32[16]{0:T(128)}, u32[]{:S(2)}) copy-start(f32[16]{0:T(128)} %get-tuple-element.151) | copy-start | bytes 196
  94.5 32.2 %copy-start.126 = (f32[16]{0:T(128)S(1)}, f32[16]{0:T(128)}, u32[]{:S(2)}) copy-start(f32[16]{0:T(128)} %get-tuple-element.152) | copy-start | bytes 196
  160.1 18.9 %copy-start.49 = (f32[16]{0:T(128)S(1)}, f32[16]{0:T(128)}, u32[]{:S(2)}) copy-start(f32[16]{0:T(128)} %get-tuple-element.261) | copy-start | bytes 196
  160.1 18.9 %copy-start.50 = (f32[16]{0:T(128)S(1)}, f32[16]{0:T(128)}, u32[]{:S(2)}) copy-start(f32[16]{0:T(128)} %get-tuple-element.277) | copy-start | bytes 196
  160.1 18.9 %copy-start.51 = (f32[16]{0:T(128)S(1)}, f32[16]{0:T(128)}, u32[]{:S(2)}) copy-start(f32[16]{0:T(128)} %get-tuple-element.278) | copy-start | bytes 196
  160.1 18.9 %copy-start.52 = (f32[16]{0:T(128)S(1)}, f32[16]{0:T(128)}, u32[]{:S(2)}) copy-start(f32[16]{0:T(128)} %get-tuple-element.279) | copy-start | bytes 196
  160.1 18.9 %copy-start.53 = (f32[16]{0:T(128)S(1)}, f32[16]{0:T(128)}, u32[]{:S(2)}) copy-start(f32[16]{0:T(128)} %get-tuple-element.280) | copy-start | bytes 196
  160.2 18.9 %copy-start.54 = (f32[16]{0:T(128)S(1)}, f32[16]{0:T(128)}, u32[]{:S(2)}) copy-start(f32[16]{0:T(128)} %get-tuple-element.281) | copy-start | bytes 196
  160.2 18.9 %copy-start.55 = (f32[16]{0:T(128)S(1)}, f32[16]{0:T(128)}, u32[]{:S(2)}) copy-start(f32[16]{0:T(128)} %get-tuple-element.282) | copy-start | bytes 196
  160.2 18.9 %copy-start.56 = (f32[16]{0:T(128)S(1)}, f32[16]{0:T(128)}, u32[]{:S(2)}) copy-start(f32[16]{0:T(128)} %get-tuple-element.283) | copy-start | bytes 196
  160.2 18.9 %copy-start.57 = (f32[16]{0:T(128)S(1)}, f32[16]{0:T(128)}, u32[]{:S(2)}) copy-start(f32[16]{0:T(128)} %get-tuple-element.284) | copy-start | bytes 196
  160.2 18.9 %copy-start.58 = (f32[16]{0:T(128)S(1)}, f32[16]{0:T(128)}, u32[]{:S(2)}) copy-start(f32[16]{0:T(128)} %get-tuple-element.285) | copy-start | bytes 196
  160.2 18.9 %copy-start.59 = (f32[16]{0:T(128)S(1)}, f32[16]{0:T(128)}, u32[]{:S(2)}) copy-start(f32[16]{0:T(128)} %get-tuple-element.286) | copy-start | bytes 196
  160.2 18.9 %copy-start.60 = (f32[16]{0:T(128)S(1)}, f32[16]{0:T(128)}, u32[]{:S(2)}) copy-start(f32[16]{0:T(128)} %get-tuple-element.287) | copy-start | bytes 196
  160.2 18.9 %copy-start.61 = (f32[16]{0:T(128)S(1)}, f32[16]{0:T(128)}, u32[]{:S(2)}) copy-start(f32[16]{0:T(128)} %get-tuple-element.288) | copy-start | bytes 196
  160.2 18.9 %copy-start.62 = (f32[16]{0:T(128)S(1)}, f32[16]{0:T(128)}, u32[]{:S(2)}) copy-start(f32[16]{0:T(128)} %get-tuple-element.289) | copy-start | bytes 196
  160.2 18.9 %copy-start.63 = (f32[16]{0:T(128)S(1)}, f32[16]{0:T(128)}, u32[]{:S(2)}) copy-start(f32[16]{0:T(128)} %get-tuple-element.290) | copy-start | bytes 196
  160.3 18.9 %copy-start.64 = (f32[16]{0:T(128)S(1)}, f32[16]{0:T(128)}, u32[]{:S(2)}) copy-start(f32[16]{0:T(128)} %get-tuple-element.291) | copy-start | bytes 196
  160.3 18.9 %copy-start.65 = (f32[16]{0:T(128)S(1)}, f32[16]{0:T(128)}, u32[]{:S(2)}) copy-start(f32[16]{0:T(128)} %get-tuple-element.292) | copy-start | bytes 196
  160.3 18.9 %copy-start.66 = (f32[16]{0:T(128)S(1)}, f32[16]{0:T(128)}, u32[]{:S(2)}) copy-start(f32[16]{0:T(128)} %get-tuple-element.293) | copy-start | bytes 196
  160.3 18.9 %copy-start.67 = (f32[16]{0:T(128)S(1)}, f32[16]{0:T(128)}, u32[]{:S(2)}) copy-start(f32[16]{0:T(128)} %get-tuple-element.294) | copy-start | bytes 196
  160.3 18.9 %copy-start.68 = (f32[16]{0:T(128)S(1)}, f32[16]{0:T(128)}, u32[]{:S(2)}) copy-start(f32[16]{0:T(128)} %get-tuple-element.295) | copy-start | bytes 196
  160.3 18.9 %copy-start.69 = (f32[16]{0:T(128)S(1)}, f32[16]{0:T(128)}, u32[]{:S(2)}) copy-start(f32[16]{0:T(128)} %get-tuple-element.296) | copy-start | bytes 196
  160.3 18.9 %copy-start.70 = (f32[16]{0:T(128)S(1)}, f32[16]{0:T(128)}, u32[]{:S(2)}) copy-start(f32[16]{0:T(128)} %get-tuple-element.297) | copy-start | bytes 196
  160.3 18.9 %copy-start.71 = (f32[16]{0:T(128)S(1)}, f32[16]{0:T(128)}, u32[]{:S(2)}) copy-start(f32[16]{0:T(128)} %get-tuple-element.298) | copy-start | bytes 196
  163.2 48.4 %all-to-all-start.1 = ((bf16[16,2,128]{2,1,0:T(2,128)(2,1)}), bf16[16,2,128]{2,1,0:T(2,128)(2,1)S(1)}, u32[]{:S(2)}, u32[]{:S(2)}) async-start(bf16[16,2,128]{2,1,0:T(2,128)(2,1)} %reshape.1243), calls=%async_computation.1 | async-start | bytes 16384 | tf_op jit(solution)/shard_map/all_to_all | solution.py:101
  178.9 457.2 %all-reduce.3.cloned.1.call-start = ((), (), s32[]{:S(2)}) async-start(), calls=%async_computation.2 | async-start | bytes 786432
  249.7 386.4 %copy-start.6 = (bf16[24,64,64]{2,1,0:T(8,128)(2,1)S(1)}, bf16[24,64,64]{2,1,0:T(8,128)(2,1)}, u32[]{:S(2)}) copy-start(bf16[24,64,64]{2,1,0:T(8,128)(2,1)} %fusion.561) | copy-start | bytes 589828
  250.2 385.9 %copy-start.7 = (bf16[24,64,64]{2,1,0:T(8,128)(2,1)S(1)}, bf16[24,64,64]{2,1,0:T(8,128)(2,1)}, u32[]{:S(2)}) copy-start(bf16[24,64,64]{2,1,0:T(8,128)(2,1)} %get-tuple-element.499) | copy-start | bytes 589828
  744.9 74.9 %copy-start.4 = (bf16[16,1,180,64]{2,3,1,0:T(8,128)(2,1)S(1)}, bf16[16,1,180,64]{2,3,1,0:T(8,128)(2,1)}, u32[]{:S(2)}) copy-start(bf16[16,1,180,64]{2,3,1,0:T(8,128)(2,1)} %copy.68) | copy-start | bytes 1105924
  744.9 74.9 %copy-start.5 = (bf16[16,1,180,64]{2,3,1,0:T(8,128)(2,1)S(1)}, bf16[16,1,180,64]{2,3,1,0:T(8,128)(2,1)}, u32[]{:S(2)}) copy-start(bf16[16,1,180,64]{2,3,1,0:T(8,128)(2,1)} %copy.69) | copy-start | bytes 1105924
  (87 other events, 434.3 us)
Sparse Core Ops, SparseCore 0:
  213.3 422.7 all-reduce.2
where the time goes:
time: 839 us; the launch traced here: 830 us
  waiting for transfers between devices  385 us (46%)
  blocking collectives  181 us (22%)
  other arithmetic  133 us (16%)
  starting transfers between devices  54.1 us (6%)
  local copies, waits for them, and re-layouts  53.6 us (6%)
  between operations  16.6 us (2%)
    unnamed x2, waiting for transfers between devices  385 us
    another operation x6, other arithmetic  131 us
    all_gather x1, blocking collectives, per_device(): portion = lax.all_gather(mixed_modes, 'lat', axis=0, tiled=True)  107 us
    all_gather x1, blocking collectives, per_device(): portion = lax.all_gather(grid_modes, 'lon', axis=1, tiled=True)  74.4 us
    slice x27, local copies, waits for them, and re-layouts, disco(): kernel_coef[:, kernel, lat_step, lon_step][:, None] * window  39.3 us
    all_to_all x1, starting transfers between devices, per_device(): lax.all_to_all(grid_field, 'lon', split_axis=0, concat_axis=1, tiled=True)  19.4 us
  transfers between devices with their start and end apart: 7, of which 1 were waited for; matrix products, arithmetic and copies ran while one was open for 22% of the time, Pallas kernels for 0%

commit v1 on v0

--- a/solution.py
+++ b/solution.py
@@ -127,7 +127,9 @@
     mixed_modes = jnp.einsum(
         "lmc,lcd->lmd", coeffs, complex_block, preferred_element_type=jnp.float32
     ).astype(jnp.bfloat16)
-    portion = lax.all_gather(mixed_modes, "lat", axis=0, tiled=True)
+    portion = jnp.concatenate(
+        lax.all_to_all(jnp.stack([mixed_modes] * lax.axis_size("lat")), "lat", 0, 0), axis=0
+    )
     grid_modes = jnp.einsum(
         "iml,lmc->imc", masked(portion.shape[0]), portion, preferred_element_type=jnp.float32
     ).astype(jnp.bfloat16)

time: 839 us -> 731 us (0.87)
  blocking collectives: 181 us -> 61 us
  starting transfers between devices: 54.1 us -> 63.8 us
    all_gather x1 -> x0, blocking collectives: 107 us -> none  [per_device(): portion = lax.all_gather(mixed_modes, 'lat', axis=0, tiled=True)]
    all_gather x1, blocking collectives: 74.4 us -> 61 us  [per_device(): portion = lax.all_gather(grid_modes, 'lon', axis=1, tiled=True)]
    all_to_all x0 -> x1, starting transfers between devices: none -> 9.51 us  [per_device(): lax.all_to_all(jnp.stack([mixed_modes] * lax.axis_size('lat')), 'lat', 0, 0)]
  transfers between devices with their start and end apart: 7 -> 8, of which waited for: 1 -> 1; matrix products, arithmetic and copies ran while one was open for 22% -> 25% of each run, Pallas kernels for 0% -> 0%
where the time goes in v1:
time: 731 us; the launch traced here: 721 us
  waiting for transfers between devices  387 us (53%)
  other arithmetic  132 us (18%)
  starting transfers between devices  63.8 us (9%)
  blocking collectives  61 us (8%)
  local copies, waits for them, and re-layouts  54.5 us (7%)
  between operations  17.2 us (2%)
    unnamed x2, waiting for transfers between devices  387 us
    another operation x6, other arithmetic  130 us
    all_gather x1, blocking collectives, per_device(): portion = lax.all_gather(grid_modes, 'lon', axis=1, tiled=True)  61 us
    slice x27, local copies, waits for them, and re-layouts, disco(): kernel_coef[:, kernel, lat_step, lon_step][:, None] * window  39.3 us
    all_to_all x1, starting transfers between devices, per_device(): lax.all_to_all(grid_field, 'lon', split_axis=0, concat_axis=1, tiled=True)  19.4 us
    all_to_all x1, starting transfers between devices, per_device(): lax.all_to_all(row_spectra, 'lon', split_axis=1, concat_axis=0, tiled=True)  15.7 us
    ppermute x2, starting transfers between devices, padded(): lax.ppermute(tail, axis, [(i, (i + 1) % count) for i in range(ends)])  15.4 us
  transfers between devices with their start and end apart: 8, of which 1 were waited for; matrix products, arithmetic and copies ran while one was open for 25% of the time, Pallas kernels for 0%

profile of v1, /device:TPU:1, one launch (start us, length us, event | category | flops | bytes accessed | tf_op | source)
XLA Modules:
  0.0 721.5 jit_solution(82374373181835394)
XLA Ops:
  6.5 19.4 %all-to-all-start = ((bf16[16,180,64]{1,2,0:T(8,128)(2,1)}), bf16[16,180,64]{1,2,0:T(8,128)(2,1)S(1)}, u32[]{:S(2)}, u32[]{:S(2)}) async-start(bf16[16,180,64]{1,2,0:T(8,128)(2,1)} %param.6), calls=%async_computation | async-start | bytes 1048576 | tf_op jit(solution)/shard_map/all_to_all | solution.py:97
  26.8 12.2 %collective-permute-start = (bf16[16,20,64]{1,2,0:T(8,128)(2,1)}, bf16[16,20,64]{1,2,0:T(8,128)(2,1)S(1)}, u32[]{:S(2)}, u32[]{:S(2)}) collective-permute-start(bf16[16,20,64]{1,2,0:T(8,128)(2,1)} %get-tuple-element.501), channel_id=1, source_target_pairs={{0,1},{1,2},{2,3},{3,4},{4,5},{5,6},{6,7},{7,8},{8,9},{9,10},{10,1... | collective-permute-start | bytes 122888 | tf_op jit(solution)/shard_map/ppermute | solution.py:20
  39.0 1.9 collective-permute-start.1
  41.3 1.5 slice_reduce_fusion.486
  42.8 1.4 slice_reduce_fusion.491
  44.2 1.5 slice_reduce_fusion.490
  45.7 1.5 slice_reduce_fusion.489
  47.2 1.5 slice_reduce_fusion.488
  48.7 1.5 slice_reduce_fusion.487
  50.1 1.3 slice_reduce_fusion.485
  51.4 1.5 slice_reduce_fusion.363
  53.0 1.5 slice_reduce_fusion.362
  54.4 1.5 slice_reduce_fusion.361
  55.9 1.5 slice_reduce_fusion.360
  57.4 1.5 slice_reduce_fusion.359
  58.9 1.4 slice_reduce_fusion.358
  60.3 1.3 slice_reduce_fusion.357
  61.6 1.5 slice_reduce_fusion.235
  63.1 1.5 slice_reduce_fusion.234
  64.6 1.7 slice_reduce_fusion.233
  66.3 1.5 slice_reduce_fusion.232
  67.7 1.5 slice_reduce_fusion.231
  69.2 1.5 slice_reduce_fusion.230
  70.7 1.5 slice_reduce_fusion.107
  72.2 1.5 slice_reduce_fusion.106
  73.7 1.5 slice_reduce_fusion.105
  75.1 1.5 slice_reduce_fusion.104
  76.6 1.5 slice_reduce_fusion.103
  78.1 2.3 multiply_convert_fusion
  82.5 1.3 slice_reduce_fusion.229
  83.9 3.1 collective-permute-start.2
  87.0 1.7 collective-permute-start.3
  88.7 1.3 slice_reduce_fusion.102
  90.0 1.3 dynamic-slice
  94.6 32.2 %fusion.533 = bf16[16,11520]{1,0:T(8,128)(2,1)S(1)} fusion(f32[16]{0:T(128)S(1)} %copy-done.145, f32[16]{0:T(128)S(1)} %copy-done.146, f32[16]{0:T(128)S(1)} %copy-done.147, f32[16]{0:T(128)S(1)} %copy-done.148, f32[16]{0:T(128)S(1)} %copy-done.149, f32[16]{0:T(128)S(1)} %copy-done.150, f32[16]{0:T(128)S(1)} %copy-done.151, f32[16]{0:T(128)S(1)} %copy-done.152, ...), kind=kLoop, calls=%fused_computation.1021 | loop fusion | flops 68014080 | bytes 45719232 | tf_op jit(solution)/shard_map/convert.8
  128.2 1.3 fusion.18
  130.2 15.7 %all-to-all-start.1 = ((bf16[16,2,128]{2,1,0:T(2,128)(2,1)}), bf16[16,2,128]{2,1,0:T(2,128)(2,1)S(1)}, u32[]{:S(2)}, u32[]{:S(2)}) async-start(bf16[16,2,128]{2,1,0:T(2,128)(2,1)} %reshape.1249), calls=%async_computation.1 | async-start | bytes 16384 | tf_op jit(solution)/shard_map/all_to_all | solution.py:101
  146.6 31.9 %fusion.532 = bf16[16,11520]{1,0:T(8,128)(2,1)S(1)} fusion(f32[16]{0:T(128)S(1)} %copy-done.87, f32[16]{0:T(128)S(1)} %copy-done.88, f32[16]{0:T(128)S(1)} %copy-done.89, f32[16]{0:T(128)S(1)} %copy-done.90, f32[16]{0:T(128)S(1)} %copy-done.91, f32[16]{0:T(128)S(1)} %copy-done.92, f32[16]{0:T(128)S(1)} %copy-done.93, f32[16]{0:T(128)S(1)} %copy-done.94, ...), kind=kLoop, calls=%fused_computation.1020 | loop fusion | flops 68014080 | bytes 45719232 | tf_op jit(solution)/shard_map/convert.7
  180.9 31.8 %fusion.531 = bf16[16,11520]{1,0:T(8,128)(2,1)S(1)} fusion(f32[16]{0:T(128)S(1)} %copy-done.48, f32[16]{0:T(128)S(1)} %copy-done.49, f32[16]{0:T(128)S(1)} %copy-done.50, f32[16]{0:T(128)S(1)} %copy-done.52, f32[16]{0:T(128)S(1)} %copy-done.53, f32[16]{0:T(128)S(1)} %copy-done.54, f32[16]{0:T(128)S(1)} %copy-done.55, f32[16]{0:T(128)S(1)} %copy-done.56, ...), kind=kLoop, calls=%fused_computation.1019 | loop fusion | flops 68014080 | bytes 45719232 | tf_op jit(solution)/shard_map/convert.6
  214.0 1.1 copy.74
  215.7 1.1 copy.75
  216.8 386.6 %all-reduce.3.cloned.1.call-done = bf16[768,2,128]{2,1,0:T(2,128)(2,1)} async-done(((bf16[768,2,128]{2,1,0:T(2,128)(2,1)}), bf16[768,2,128]{2,1,0:T(2,128)(2,1)}) %all-reduce.3.cloned.1.call-update) | async-done | bytes 393232
  603.4 1.8 convolution_convert_fusion.2
  606.3 9.5 %all-to-all-start.2 = ((bf16[32,24,2,128]{3,1,2,0:T(8,128)(2,1)}), bf16[32,24,2,128]{3,1,2,0:T(8,128)(2,1)S(1)}, u32[]{:S(2)}, u32[]{:S(2)}) async-start(bf16[32,24,2,128]{3,1,2,0:T(8,128)(2,1)} %stack.20), calls=%async_computation.2 | async-start | bytes 786432 | tf_op jit(solution)/shard_map/all_to_all | solution.py:131
  616.2 31.6 %fusion.530 = bf16[16,11520]{1,0:T(8,128)(2,1)S(1)} fusion(f32[16]{0:T(128)S(1)} %copy-done.8, f32[16]{0:T(128)S(1)} %copy-done.9, f32[16]{0:T(128)S(1)} %copy-done.10, f32[16]{0:T(128)S(1)} %copy-done.11, f32[16]{0:T(128)S(1)} %copy-done.12, f32[16]{0:T(128)S(1)} %copy-done.13, f32[16]{0:T(128)S(1)} %copy-done.14, f32[16]{0:T(128)S(1)} %copy-done.15, ...), kind=kLoop, calls=%fused_computation.1018 | loop fusion | flops 68014080 | bytes 45719232 | tf_op jit(solution)/shard_map/convert.5
  648.3 1.2 copy.76
  649.7 61.0 %all_gather.3 = bf16[16,32,128]{2,0,1:T(8,128)(2,1)S(1)} all-gather(bf16[16,2,128]{2,0,1:T(8,128)(2,1)S(1)} %fusion.19), channel_id=1, replica_groups=mesh['lat'=32,'lon'=16] {'lon'}, dimensions={1}, use_global_device_ids=true | all-gather | bytes 139264 | tf_op jit(solution)/shard_map/all_gather | solution.py:137
  711.3 2.9 fusion.32
  (372 shorter events, 13.3 us)
Async XLA Ops:
  6.5 704.7 %copy-start = (bf16[4,64,64]{2,1,0:T(8,128)(2,1)S(1)}, bf16[4,64,64]{2,1,0:T(8,128)(2,1)}, u32[]{:S(2)}) copy-start(bf16[4,64,64]{2,1,0:T(8,128)(2,1)} %param.9) | copy-start | bytes 98308
  6.5 19.4 %copy-start.1 = (bf16[16,180,64]{1,2,0:T(8,128)(2,1)S(1)}, bf16[16,180,64]{1,2,0:T(8,128)(2,1)}, u32[]{:S(2)}) copy-start(bf16[16,180,64]{1,2,0:T(8,128)(2,1)} %param.6) | copy-start | bytes 1105924
  6.5 34.4 %copy-start.7 = (f32[16,492]{1,0:T(8,128)S(1)}, f32[16,492]{1,0:T(8,128)}, u32[]{:S(2)}) copy-start(f32[16,492]{1,0:T(8,128)} %param.8) | copy-start | bytes 94468
  6.5 34.6 %copy-start.163 = (s32[16]{0:T(128)S(1)}, s32[16]{0:T(128)}, u32[]{:S(2)}) copy-start(s32[16]{0:T(128)} %param.7) | copy-start | bytes 196
  6.5 120.3 %all-to-all-start = ((bf16[16,180,64]{1,2,0:T(8,128)(2,1)}), bf16[16,180,64]{1,2,0:T(8,128)(2,1)S(1)}, u32[]{:S(2)}, u32[]{:S(2)}) async-start(bf16[16,180,64]{1,2,0:T(8,128)(2,1)} %param.6), calls=%async_computation | async-start | bytes 1048576 | tf_op jit(solution)/shard_map/all_to_all | solution.py:97
  26.8 57.0 %collective-permute-start = (bf16[16,20,64]{1,2,0:T(8,128)(2,1)}, bf16[16,20,64]{1,2,0:T(8,128)(2,1)S(1)}, u32[]{:S(2)}, u32[]{:S(2)}) collective-permute-start(bf16[16,20,64]{1,2,0:T(8,128)(2,1)} %get-tuple-element.501), channel_id=1, source_target_pairs={{0,1},{1,2},{2,3},{3,4},{4,5},{5,6},{6,7},{7,8},{8,9},{9,10},{10,1... | collective-permute-start | bytes 122888 | tf_op jit(solution)/shard_map/ppermute | solution.py:20
  39.0 44.8 %collective-permute-start.1 = (bf16[16,20,64]{1,2,0:T(8,128)(2,1)S(1)}, bf16[16,20,64]{1,2,0:T(8,128)(2,1)S(1)}, u32[]{:S(2)}, u32[]{:S(2)}) collective-permute-start(bf16[16,20,64]{1,2,0:T(8,128)(2,1)S(1)} %get-tuple-element.502), channel_id=1, source_target_pairs={{1,0},{2,1},{3,2},{4,3},{5,4},{6,5},{7,6},{8,7},{9,8},{10,9},{11,1... | collective-permute-start | bytes 122888 | tf_op jit(solution)/shard_map/ppermute | solution.py:22
  83.9 8.0 %collective-permute-start.2 = (bf16[1,220,64]{1,2,0:T(8,128)(2,1)S(1)}, bf16[1,220,64]{1,2,0:T(8,128)(2,1)S(1)}, u32[]{:S(2)}, u32[]{:S(2)}) collective-permute-start(bf16[1,220,64]{1,2,0:T(8,128)(2,1)S(1)} %get-tuple-element.497), channel_id=1, source_target_pairs={{0,16},{16,32},{32,48},{48,64},{64,80},{80,96},{96,112},{112,128},... | collective-permute-start | bytes 84488 | tf_op jit(solution)/shard_map/ppermute | solution.py:20
  87.0 4.9 collective-permute-start.3
  127.1 19.0 %copy-start.86 = (f32[16]{0:T(128)S(1)}, f32[16]{0:T(128)}, u32[]{:S(2)}) copy-start(f32[16]{0:T(128)} %get-tuple-element.133) | copy-start | bytes 196
  127.1 19.0 %copy-start.87 = (f32[16]{0:T(128)S(1)}, f32[16]{0:T(128)}, u32[]{:S(2)}) copy-start(f32[16]{0:T(128)} %get-tuple-element.144) | copy-start | bytes 196
  127.1 19.0 %copy-start.88 = (f32[16]{0:T(128)S(1)}, f32[16]{0:T(128)}, u32[]{:S(2)}) copy-start(f32[16]{0:T(128)} %get-tuple-element.145) | copy-start | bytes 196
  127.2 19.0 %copy-start.89 = (f32[16]{0:T(128)S(1)}, f32[16]{0:T(128)}, u32[]{:S(2)}) copy-start(f32[16]{0:T(128)} %get-tuple-element.146) | copy-start | bytes 196
  127.2 19.0 %copy-start.90 = (f32[16]{0:T(128)S(1)}, f32[16]{0:T(128)}, u32[]{:S(2)}) copy-start(f32[16]{0:T(128)} %get-tuple-element.147) | copy-start | bytes 196
  127.2 19.0 %copy-start.91 = (f32[16]{0:T(128)S(1)}, f32[16]{0:T(128)}, u32[]{:S(2)}) copy-start(f32[16]{0:T(128)} %get-tuple-element.148) | copy-start | bytes 196
  127.2 19.0 %copy-start.92 = (f32[16]{0:T(128)S(1)}, f32[16]{0:T(128)}, u32[]{:S(2)}) copy-start(f32[16]{0:T(128)} %get-tuple-element.149) | copy-start | bytes 196
  127.2 19.0 %copy-start.93 = (f32[16]{0:T(128)S(1)}, f32[16]{0:T(128)}, u32[]{:S(2)}) copy-start(f32[16]{0:T(128)} %get-tuple-element.150) | copy-start | bytes 196
  127.2 19.0 %copy-start.94 = (f32[16]{0:T(128)S(1)}, f32[16]{0:T(128)}, u32[]{:S(2)}) copy-start(f32[16]{0:T(128)} %get-tuple-element.151) | copy-start | bytes 196
  127.2 19.0 %copy-start.95 = (f32[16]{0:T(128)S(1)}, f32[16]{0:T(128)}, u32[]{:S(2)}) copy-start(f32[16]{0:T(128)} %get-tuple-element.152) | copy-start | bytes 196
  127.2 19.0 %copy-start.96 = (f32[16]{0:T(128)S(1)}, f32[16]{0:T(128)}, u32[]{:S(2)}) copy-start(f32[16]{0:T(128)} %get-tuple-element.153) | copy-start | bytes 196
  127.2 19.0 %copy-start.97 = (f32[16]{0:T(128)S(1)}, f32[16]{0:T(128)}, u32[]{:S(2)}) copy-start(f32[16]{0:T(128)} %get-tuple-element.154) | copy-start | bytes 196
  127.2 19.0 %copy-start.98 = (f32[16]{0:T(128)S(1)}, f32[16]{0:T(128)}, u32[]{:S(2)}) copy-start(f32[16]{0:T(128)} %get-tuple-element.155) | copy-start | bytes 196
  127.3 19.0 %copy-start.99 = (f32[16]{0:T(128)S(1)}, f32[16]{0:T(128)}, u32[]{:S(2)}) copy-start(f32[16]{0:T(128)} %get-tuple-element.156) | copy-start | bytes 196
  127.3 19.0 %copy-start.100 = (f32[16]{0:T(128)S(1)}, f32[16]{0:T(128)}, u32[]{:S(2)}) copy-start(f32[16]{0:T(128)} %get-tuple-element.157) | copy-start | bytes 196
  127.3 19.0 %copy-start.101 = (f32[16]{0:T(128)S(1)}, f32[16]{0:T(128)}, u32[]{:S(2)}) copy-start(f32[16]{0:T(128)} %get-tuple-element.158) | copy-start | bytes 196
  127.3 19.0 %copy-start.102 = (f32[16]{0:T(128)S(1)}, f32[16]{0:T(128)}, u32[]{:S(2)}) copy-start(f32[16]{0:T(128)} %get-tuple-element.159) | copy-start | bytes 196
  127.3 19.0 %copy-start.103 = (f32[16]{0:T(128)S(1)}, f32[16]{0:T(128)}, u32[]{:S(2)}) copy-start(f32[16]{0:T(128)} %get-tuple-element.160) | copy-start | bytes 196
  127.3 19.0 %copy-start.104 = (f32[16]{0:T(128)S(1)}, f32[16]{0:T(128)}, u32[]{:S(2)}) copy-start(f32[16]{0:T(128)} %get-tuple-element.161) | copy-start | bytes 196
  127.3 19.0 %copy-start.105 = (f32[16]{0:T(128)S(1)}, f32[16]{0:T(128)}, u32[]{:S(2)}) copy-start(f32[16]{0:T(128)} %get-tuple-element.162) | copy-start | bytes 196
  127.3 19.0 %copy-start.106 = (f32[16]{0:T(128)S(1)}, f32[16]{0:T(128)}, u32[]{:S(2)}) copy-start(f32[16]{0:T(128)} %get-tuple-element.163) | copy-start | bytes 196
  127.3 19.0 %copy-start.107 = (f32[16]{0:T(128)S(1)}, f32[16]{0:T(128)}, u32[]{:S(2)}) copy-start(f32[16]{0:T(128)} %get-tuple-element.164) | copy-start | bytes 196
  127.3 19.0 %copy-start.108 = (f32[16]{0:T(128)S(1)}, f32[16]{0:T(128)}, u32[]{:S(2)}) copy-start(f32[16]{0:T(128)} %get-tuple-element.165) | copy-start | bytes 196
  127.4 19.0 %copy-start.109 = (f32[16]{0:T(128)S(1)}, f32[16]{0:T(128)}, u32[]{:S(2)}) copy-start(f32[16]{0:T(128)} %get-tuple-element.166) | copy-start | bytes 196
  127.4 19.0 %copy-start.110 = (f32[16]{0:T(128)S(1)}, f32[16]{0:T(128)}, u32[]{:S(2)}) copy-start(f32[16]{0:T(128)} %get-tuple-element.167) | copy-start | bytes 196
  127.4 19.0 %copy-start.111 = (f32[16]{0:T(128)S(1)}, f32[16]{0:T(128)}, u32[]{:S(2)}) copy-start(f32[16]{0:T(128)} %get-tuple-element.168) | copy-start | bytes 196
  127.4 19.0 %copy-start.112 = (f32[16]{0:T(128)S(1)}, f32[16]{0:T(128)}, u32[]{:S(2)}) copy-start(f32[16]{0:T(128)} %get-tuple-element.169) | copy-start | bytes 196
  127.4 19.0 %copy-start.113 = (f32[16]{0:T(128)S(1)}, f32[16]{0:T(128)}, u32[]{:S(2)}) copy-start(f32[16]{0:T(128)} %get-tuple-element.170) | copy-start | bytes 196
  127.4 19.0 %copy-start.114 = (f32[16]{0:T(128)S(1)}, f32[16]{0:T(128)}, u32[]{:S(2)}) copy-start(f32[16]{0:T(128)} %get-tuple-element.171) | copy-start | bytes 196
  127.4 19.0 %copy-start.115 = (f32[16]{0:T(128)S(1)}, f32[16]{0:T(128)}, u32[]{:S(2)}) copy-start(f32[16]{0:T(128)} %get-tuple-element.172) | copy-start | bytes 196
  127.4 19.0 %copy-start.116 = (f32[16]{0:T(128)S(1)}, f32[16]{0:T(128)}, u32[]{:S(2)}) copy-start(f32[16]{0:T(128)} %get-tuple-element.173) | copy-start | bytes 196
  127.4 19.0 %copy-start.117 = (f32[16]{0:T(128)S(1)}, f32[16]{0:T(128)}, u32[]{:S(2)}) copy-start(f32[16]{0:T(128)} %get-tuple-element.174) | copy-start | bytes 196
  127.4 19.0 %copy-start.118 = (f32[16]{0:T(128)S(1)}, f32[16]{0:T(128)}, u32[]{:S(2)}) copy-start(f32[16]{0:T(128)} %get-tuple-element.175) | copy-start | bytes 196
  130.2 48.7 %all-to-all-start.1 = ((bf16[16,2,128]{2,1,0:T(2,128)(2,1)}), bf16[16,2,128]{2,1,0:T(2,128)(2,1)S(1)}, u32[]{:S(2)}, u32[]{:S(2)}) async-start(bf16[16,2,128]{2,1,0:T(2,128)(2,1)} %reshape.1249), calls=%async_computation.1 | async-start | bytes 16384 | tf_op jit(solution)/shard_map/all_to_all | solution.py:101
  145.9 457.4 %all-reduce.3.cloned.1.call-start = ((), (), s32[]{:S(2)}) async-start(), calls=%async_computation.3 | async-start | bytes 786432
  215.7 387.7 %copy-start.5 = (bf16[24,64,64]{2,1,0:T(8,128)(2,1)S(1)}, bf16[24,64,64]{2,1,0:T(8,128)(2,1)}, u32[]{:S(2)}) copy-start(bf16[24,64,64]{2,1,0:T(8,128)(2,1)} %fusion.560) | copy-start | bytes 589828
  606.3 43.2 %all-to-all-start.2 = ((bf16[32,24,2,128]{3,1,2,0:T(8,128)(2,1)}), bf16[32,24,2,128]{3,1,2,0:T(8,128)(2,1)S(1)}, u32[]{:S(2)}, u32[]{:S(2)}) async-start(bf16[32,24,2,128]{3,1,2,0:T(8,128)(2,1)} %stack.20), calls=%async_computation.2 | async-start | bytes 786432 | tf_op jit(solution)/shard_map/all_to_all | solution.py:131
  649.7 61.6 %copy-start.3 = (bf16[16,1,180,64]{2,3,1,0:T(8,128)(2,1)S(1)}, bf16[16,1,180,64]{2,3,1,0:T(8,128)(2,1)}, u32[]{:S(2)}) copy-start(bf16[16,1,180,64]{2,3,1,0:T(8,128)(2,1)} %copy.74) | copy-start | bytes 1105924
  649.7 61.6 %copy-start.4 = (bf16[16,1,180,64]{2,3,1,0:T(8,128)(2,1)S(1)}, bf16[16,1,180,64]{2,3,1,0:T(8,128)(2,1)}, u32[]{:S(2)}) copy-start(bf16[16,1,180,64]{2,3,1,0:T(8,128)(2,1)} %copy.75) | copy-start | bytes 1105924
  (124 other events, 677.8 us)
Sparse Core Ops, SparseCore 0:
  180.6 422.7 all-reduce.2
